TPU v7x, 32 devices: a whole 2x2x4 slice. The times are simulated.
32 devices in a mesh: band: 8 (over y, x, core), head: 4 (over z).
Axes of the slice: x: 2, y: 2, z: 4, core: 2. Of those that a mesh axis runs over, the one named last changes fastest.
Arguments:
- queries: bfloat16 [1024, 1536], P('band', 'head'), as said below
- keys: bfloat16 [1024, 1536], P('band', 'head'), as said below
- values: bfloat16 [1024, 1536], P('band', 'head'), may hold values from -6 to 6
- d_out: bfloat16 [1024, 1536], P('band', 'head'), may hold values from -6 to 6
- gain: float32 [1536], P('head'), may hold values from 0.1 to 1.9
- blocks_on: int32 [8, 4], P('band'), may hold values 0 or 1
Outputs:
- out: bfloat16 [1024, 1536], P('band', 'head')
- d_queries: bfloat16 [1024, 1536], P('band', 'head')
- d_keys: bfloat16 [1024, 1536], P('band', 'head')
- d_values: bfloat16 [1024, 1536], P('band', 'head')
Inputs may be any that keep to these rules, and one draw needn't show every extreme that they name: `queries`: entries lie within -180 to 180. `keys`: entries lie within -6 to 6.
All inputs are finite; a program needn't handle non-finite values. No bound on the sum of `blocks_on` on one device may be relied on, other than what follows from the above.
Results may differ from a plain program's by a relative error of at most 0.0063.
Values may be sent and summed in bfloat16 or wider, within the bound.
No kernel may reach another device: no remote copies, remote signals or barrier semaphores. Data moves between devices by JAX's collectives and lax.ppermute only.
A program may use at most 64 MiB of HBM per device.

v0:
```python
import functools

import jax
import jax.numpy as jnp
from jax import lax
from jax.experimental import pallas as pl
from jax.experimental.pallas import tpu as pltpu
from jax.sharding import PartitionSpec as P

HEAD_DIM = 128
NEG = -1e30
EPS = 1e-06
SCALING = HEAD_DIM ** (-0.5)
STAT_ROWS = 16
F32 = jnp.float32
BF16 = jnp.bfloat16
VMEM_BYTES = 24 * 1024 * 1024


def matmul_nt(left, right):
    return lax.dot_general(left, right, (((1,), (1,)), ((), ())), preferred_element_type=F32)


def matmul(left, right):
    return jnp.dot(left, right, preferred_element_type=F32)


def head_slice(h):
    return slice(h * HEAD_DIM, (h + 1) * HEAD_DIM)


def to_lanes(columns, rows):
    lane = lax.broadcasted_iota(jnp.int32, (rows, HEAD_DIM), 1)
    packed = jnp.zeros((rows, HEAD_DIM), F32)
    for i, column in enumerate(columns):
        packed = jnp.where(lane == i, column, packed)
    return packed


def three_parts(row):
    high = row.astype(BF16).astype(F32)
    mid = (row - high).astype(BF16).astype(F32)
    low = row - high - mid
    return [high, mid, low]


def neighbour_flags(flags_ref, spacing, blocks):
    position = lax.axis_index("band")
    flags = []
    for slot, offset in enumerate((-2 * spacing, -spacing, spacing, 2 * spacing)):
        target = position + offset
        flags.append((target >= 0) & (target < blocks) & (flags_ref[0, slot] == 1))
    return flags


def is_even(spacing):
    step = lax.div(lax.axis_index("band"), spacing)
    return lax.rem(step, 2) == 0, lax.rem(lax.div(step, 2), 2) == 0


def slot_flags(flags_ref, spacing, blocks):
    m2, m1, p1, p2 = [f.astype(jnp.int32) for f in neighbour_flags(flags_ref, spacing, blocks)]
    first, even = is_even(spacing)
    return [
        None,
        jnp.where(first, p1, m1) == 1,
        jnp.where(even, p2, m2) == 1,
        jnp.where(even, m2, p2) == 1,
        jnp.where(first, m1, p1) == 1,
    ]


def masked_scores(q, keys, flags):
    scores = matmul_nt(q, jnp.concatenate(keys, axis=0)) * SCALING
    n = keys[0].shape[0]
    return [
        scores[:, j * n : (j + 1) * n]
        if flag is None
        else jnp.where(flag, scores[:, j * n : (j + 1) * n], NEG)
        for j, flag in enumerate(flags)
    ]


def forward_kernel(
    spacing, blocks, flags_ref, q_ref, g_ref, gain_ref, own, partner, inner, outer, fifth,
    attn_ref, cols_ref, stats_ref,
):
    rows = q_ref.shape[0]
    heads = q_ref.shape[1] // HEAD_DIM
    flags = slot_flags(flags_ref, spacing, blocks)
    held = [own, partner, inner, outer, fifth]
    square = jnp.zeros((rows, HEAD_DIM), F32)
    along = jnp.zeros((rows, HEAD_DIM), F32)
    peaks, inverse_totals = [], []
    for h in range(heads):
        sl = head_slice(h)
        scores = masked_scores(
            q_ref[:, sl], [r[0, :, sl] for r in held], flags
        )
        peak = functools.reduce(jnp.maximum, scores)
        peak = jnp.max(peak, axis=1, keepdims=True)
        exps = [jnp.exp(s - peak) for s in scores]
        total = jnp.sum(functools.reduce(jnp.add, exps), axis=1, keepdims=True)
        inverse_total = 1.0 / total
        weights = [(e * inverse_total).astype(BF16) for e in exps]
        attn = matmul(
            jnp.concatenate(weights, axis=1),
            jnp.concatenate([r[1, :, sl] for r in held], axis=0),
        ).astype(BF16)
        attn_ref[:, sl] = attn
        wide = attn.astype(F32)
        square = square + wide * wide
        along = along + g_ref[:, sl].astype(F32) * gain_ref[:, sl] * wide
        peaks.append(peak)
        inverse_totals.append(inverse_total)
    cols = to_lanes(
        peaks
        + inverse_totals
        + [jnp.sum(square, axis=1, keepdims=True), jnp.sum(along, axis=1, keepdims=True)],
        rows,
    )
    cols_ref[...] = cols
    stats_ref[...] = cols.T[: stats_ref.shape[0]]


def message_kernel(
    width, n_parts, *refs
):
    flags_ref, attn_ref, g_ref, gain_ref = refs[:4]
    part_refs = refs[4 : 4 + n_parts]
    msg_ref, cols_ref = refs[4 + n_parts :]
    rows = attn_ref.shape[0]
    heads = attn_ref.shape[1] // HEAD_DIM
    own = part_refs[0][...]
    total = functools.reduce(jnp.add, [r[...] for r in part_refs])
    square = total[2 * heads : 2 * heads + 1]
    along = total[2 * heads + 1 : 2 * heads + 2]
    inverse = lax.rsqrt(square / width + EPS)
    second = inverse * inverse * inverse * along / width
    sub = lax.broadcasted_iota(jnp.int32, (HEAD_DIM, rows), 0)
    packed = jnp.where(sub == 0, inverse, jnp.where(sub == 1, second, 0.0)).T
    inverse_col = packed[:, 0:1]
    second_col = packed[:, 1:2]
    deltas = []
    for h in range(heads):
        sl = head_slice(h)
        wide = attn_ref[:, sl].astype(F32)
        d_attn = (
            inverse_col * (g_ref[:, sl].astype(F32) * gain_ref[:, sl]) - wide * second_col
        ).astype(BF16)
        msg_ref[:rows, sl] = d_attn
        deltas.append(jnp.sum(d_attn.astype(F32) * wide, axis=1, keepdims=True))
    cols = to_lanes(deltas + [inverse_col], rows)
    cols_ref[...] = cols
    delta_rows = cols.T
    sub16 = lax.broadcasted_iota(jnp.int32, (STAT_ROWS, rows), 0)
    for h in range(heads):
        lines = (
            three_parts(own[h : h + 1])
            + three_parts(own[heads + h : heads + h + 1])
            + three_parts(delta_rows[h : h + 1])
        )
        block = jnp.zeros((STAT_ROWS, rows), F32)
        for i, line in enumerate(lines):
            block = jnp.where(sub16 == i, line, block)
        for slot in range(4):
            on = jnp.where(flags_ref[0, slot] == 1, 1.0, 0.0)
            block = jnp.where(sub16 == len(lines) + slot, on, block)
        msg_ref[rows:, head_slice(h)] = block.astype(BF16)


def query_kernel(
    spacing, blocks, flags_ref, q_ref, gain_ref, attn_ref, msg_ref, cols_ref, cols2_ref,
    own, partner, inner, outer, fifth, out_ref, dq_ref,
):
    rows = q_ref.shape[0]
    heads = q_ref.shape[1] // HEAD_DIM
    flags = slot_flags(flags_ref, spacing, blocks)
    held = [own, partner, inner, outer, fifth]
    inverse = cols2_ref[:, heads : heads + 1]
    for h in range(heads):
        sl = head_slice(h)
        out_ref[:, sl] = (attn_ref[:, sl].astype(F32) * inverse * gain_ref[:, sl]).astype(BF16)
        keys = [r[0, :, sl] for r in held]
        scores = masked_scores(q_ref[:, sl], keys, flags)
        peak = cols_ref[:, h : h + 1]
        inverse_total = cols_ref[:, heads + h : heads + h + 1]
        delta = cols2_ref[:, h : h + 1]
        d_weights = matmul_nt(
            msg_ref[:rows, sl],
            jnp.concatenate([r[1, :, sl] for r in held], axis=0),
        )
        d_scores = [
            (jnp.exp(s - peak) * inverse_total * (d_weights[:, j * rows : (j + 1) * rows] - delta)).astype(BF16)
            for j, s in enumerate(scores)
        ]
        dq = matmul(jnp.concatenate(d_scores, axis=1), jnp.concatenate(keys, axis=0)) * SCALING
        dq_ref[:, sl] = dq.astype(BF16)


def key_kernel(spacing, own, q0, q1, q2, q3, q4, m0, m1, m2, m3, m4, dk_ref, dv_ref):
    rows = own.shape[1]
    heads = own.shape[2] // HEAD_DIM
    first, even = is_even(spacing)
    q_refs = [q0, q1, q2, q3, q4]
    m_refs = [m0, m1, m2, m3, m4]
    for h in range(heads):
        sl = head_slice(h)
        queries = jnp.concatenate([r[:, sl] for r in q_refs], axis=0)
        d_attn = jnp.concatenate([r[:rows, sl] for r in m_refs], axis=0)
        scores = matmul_nt(own[0, :, sl], queries) * SCALING
        d_weights = matmul_nt(own[1, :, sl], d_attn)
        weights, d_scores = [], []
        for j, m_ref in enumerate(m_refs):
            stats = m_ref[rows:, sl].astype(F32)
            peak = stats[0:1] + stats[1:2] + stats[2:3]
            inverse_total = stats[3:4] + stats[4:5] + stats[5:6]
            delta = stats[6:7] + stats[7:8] + stats[8:9]
            score = scores[:, j * rows : (j + 1) * rows]
            if j > 0:
                at_m2, at_m1, at_p1, at_p2 = [stats[9 + i : 10 + i] for i in range(4)]
                flag = [
                    None,
                    jnp.where(first, at_m1, at_p1),
                    jnp.where(even, at_m2, at_p2),
                    jnp.where(even, at_p2, at_m2),
                    jnp.where(first, at_p1, at_m1),
                ][j]
                score = jnp.where(flag > 0.5, score, NEG)
            weight = jnp.exp(score - peak) * inverse_total
            weights.append(weight.astype(BF16))
            d_scores.append(
                (weight * (d_weights[:, j * rows : (j + 1) * rows] - delta)).astype(BF16)
            )
        dv_ref[:, sl] = matmul(jnp.concatenate(weights, axis=1), d_attn).astype(BF16)
        dk_ref[:, sl] = (matmul(jnp.concatenate(d_scores, axis=1), queries) * SCALING).astype(BF16)


def call(kernel, name, out_shape, args, smem_first=True):
    specs = [pl.BlockSpec(memory_space=pltpu.VMEM) for _ in args]
    if smem_first:
        specs[0] = pl.BlockSpec(memory_space=pltpu.SMEM)
    return pl.pallas_call(
        kernel,
        name=name,
        out_shape=out_shape,
        in_specs=specs,
        out_specs=jax.tree.map(lambda _: pl.BlockSpec(memory_space=pltpu.VMEM), out_shape),
        compiler_params=pltpu.CompilerParams(vmem_limit_bytes=VMEM_BYTES),
    )(*args)


def pairs_of(blocks, spacing):
    partner, inner, outer = [], [], []
    for i in range(blocks):
        step = i // spacing
        partner.append((i, i + spacing if step % 2 == 0 else i - spacing))
        to = 2 * spacing if (step // 2) % 2 == 0 else -2 * spacing
        if 0 <= i + to < blocks:
            inner.append((i, i + to))
        if 0 <= i - to < blocks:
            outer.append((i, i - to))
    return partner, inner, outer


def head_sum_parts(stats, devices):
    parts = [stats]
    for k in range(1, devices):
        if devices & (devices - 1) == 0:
            pairs = [(i, i ^ k) for i in range(devices)]
        else:
            pairs = [(i, (i + k) % devices) for i in range(devices)]
        parts.append(lax.ppermute(stats, "head", pairs))
    return parts


def local(queries, keys, values, d_out, gain, blocks_on):
    rows, width_here = queries.shape
    blocks = lax.axis_size("band")
    head_devices = lax.axis_size("head")
    spacing = blocks // 8
    heads = width_here // HEAD_DIM
    width = width_here * head_devices
    gain = gain[None, :]
    shape = jax.ShapeDtypeStruct
    partner_pairs, inner_pairs, outer_pairs = pairs_of(blocks, spacing)
    first, even = is_even(spacing)

    def swaps(array):
        outer = lax.ppermute(array, "band", outer_pairs)
        inner = lax.ppermute(array, "band", inner_pairs)
        return array, lax.ppermute(array, "band", partner_pairs), inner, outer

    def with_fifth(held):
        passed = lax.select(first == even, held[2], held[3])
        return tuple(held) + (lax.ppermute(passed, "band", partner_pairs),)

    kv = swaps(jnp.stack([keys, values]))
    qs = swaps(queries)
    kv = with_fifth(kv)

    attn, cols, stats = call(
        functools.partial(forward_kernel, spacing, blocks),
        "attention",
        (
            shape((rows, width_here), BF16),
            shape((rows, HEAD_DIM), F32),
            shape((2 * heads + 2, HEAD_DIM), F32),
        ),
        (blocks_on, queries, d_out, gain) + kv,
    )
    parts = head_sum_parts(stats, head_devices)
    qs, parts = lax.optimization_barrier((qs, parts))
    qs = with_fifth(qs)
    msg, cols2 = call(
        functools.partial(message_kernel, width, head_devices),
        "attention_gradient",
        (shape((rows + STAT_ROWS, width_here), BF16), shape((rows, HEAD_DIM), F32)),
        (blocks_on, attn, d_out, gain) + tuple(parts),
    )
    msgs = swaps(msg)
    out, d_queries = call(
        functools.partial(query_kernel, spacing, blocks),
        "query_gradient",
        (shape((rows, width_here), BF16),) * 2,
        (blocks_on, queries, gain, attn, msg, cols, cols2) + kv,
    )
    msgs, d_queries = lax.optimization_barrier((msgs, d_queries))
    msgs = with_fifth(msgs)
    d_keys, d_values = call(
        functools.partial(key_kernel, spacing),
        "key_gradient",
        (shape((rows, width_here), BF16),) * 2,
        (kv[0],) + qs + msgs,
        smem_first=False,
    )
    return out, d_queries, d_keys, d_values


def solution(mesh):
    in_specs = (
        P("band", "head"),
        P("band", "head"),
        P("band", "head"),
        P("band", "head"),
        P("head"),
        P("band", None),
    )
    out_specs = (P("band", "head"), P("band", "head"), P("band", "head"), P("band", "head"))
    return jax.shard_map(local, mesh=mesh, in_specs=in_specs, out_specs=out_specs, check_vma=False)
```

profile of v0, /device:TPU:5, one launch (start us, length us, event | category | flops | bytes accessed | tf_op | source)
XLA Modules:
  0.0 42.1 jit_solution(8701795426259931530)
XLA Ops:
  0.6 1.0 %pad_maximum_fusion.own = bf16[2,128,384]{2,1,0:T(8,128)(2,1)S(1)} fusion(bf16[1,128,384]{2,1,0:T(8,128)(2,1)} %bitcast.2, bf16[1,128,384]{2,1,0:T(8,128)(2,1)} %bitcast.3), kind=kLoop, calls=%fused_computation | loop fusion | flops 98304 | bytes 393216 | tf_op jit(solution)/shard_map/stack | solution.py:298
  1.6 1.3 %collective-permute-start.1 = (bf16[2,128,384]{2,1,0:T(8,128)(2,1)S(1)}, bf16[2,128,384]{2,1,0:T(8,128)(2,1)S(1)}, u32[]{:S(2)}, u32[]{:S(2)}) collective-permute-start(bf16[2,128,384]{2,1,0:T(8,128)(2,1)S(1)} %pad_maximum_fusion.own), channel_id=1, source_target_pairs={{0,8},{4,12},{8,0},{12,4},{16,24},{20,28},{24,16},{28,20},{1,9},{5... | collective-permute-start | bytes 589832 | tf_op jit(solution)/shard_map/ppermute | solution.py:291
  2.9 1.9 %collective-permute-start.2 = (bf16[2,128,384]{2,1,0:T(8,128)(2,1)S(1)}, bf16[2,128,384]{2,1,0:T(8,128)(2,1)S(1)}, u32[]{:S(2)}, u32[]{:S(2)}) collective-permute-start(bf16[2,128,384]{2,1,0:T(8,128)(2,1)S(1)} %pad_maximum_fusion.own), channel_id=1, source_target_pairs={{8,16},{12,20},{16,8},{20,12},{9,17},{13,21},{17,9},{21,13},{10,18... | collective-permute-start | bytes 589832 | tf_op jit(solution)/shard_map/ppermute | solution.py:290
  4.8 1.0 %collective-permute-start = (bf16[2,128,384]{2,1,0:T(8,128)(2,1)S(1)}, bf16[2,128,384]{2,1,0:T(8,128)(2,1)S(1)}, u32[]{:S(2)}, u32[]{:S(2)}) collective-permute-start(bf16[2,128,384]{2,1,0:T(8,128)(2,1)S(1)} %pad_maximum_fusion.own), channel_id=1, source_target_pairs={{0,4},{4,0},{8,12},{12,8},{16,20},{20,16},{24,28},{28,24},{1,5},{5... | collective-permute-start | bytes 589832 | tf_op jit(solution)/shard_map/ppermute | solution.py:292
  5.8 1.6 %collective-permute-done.1.inner = bf16[2,128,384]{2,1,0:T(8,128)(2,1)S(1)} collective-permute-done((bf16[2,128,384]{2,1,0:T(8,128)(2,1)S(1)}, bf16[2,128,384]{2,1,0:T(8,128)(2,1)S(1)}, u32[]{:S(2)}, u32[]{:S(2)}) %collective-permute-start.1) | collective-permute-done | bytes 196640 | tf_op jit(solution)/shard_map/ppermute | solution.py:291
  7.4 3.7 %collective-permute-done.2.outer = bf16[2,128,384]{2,1,0:T(8,128)(2,1)S(1)} collective-permute-done((bf16[2,128,384]{2,1,0:T(8,128)(2,1)S(1)}, bf16[2,128,384]{2,1,0:T(8,128)(2,1)S(1)}, u32[]{:S(2)}, u32[]{:S(2)}) %collective-permute-start.2) | collective-permute-done | bytes 196640 | tf_op jit(solution)/shard_map/ppermute | solution.py:290
  11.2 1.9 %collective-permute-start.3 = (bf16[2,128,384]{2,1,0:T(8,128)(2,1)S(1)}, bf16[2,128,384]{2,1,0:T(8,128)(2,1)S(1)}, u32[]{:S(2)}, u32[]{:S(2)}) collective-permute-start(bf16[2,128,384]{2,1,0:T(8,128)(2,1)S(1)} %broadcast_select_fusion), channel_id=1, source_target_pairs={{0,4},{4,0},{8,12},{12,8},{16,20},{20,16},{24,28},{28,24},{1,5},{5... | collective-permute-start | bytes 589832 | tf_op jit(solution)/shard_map/ppermute | solution.py:296
  13.1 0.1 collective-permute-start.4
  13.2 4.2 %collective-permute-start.6 = (bf16[128,384]{1,0:T(8,128)(2,1)S(1)}, bf16[128,384]{1,0:T(8,128)(2,1)S(1)}, u32[]{:S(2)}, u32[]{:S(2)}) collective-permute-start(bf16[128,384]{1,0:T(8,128)(2,1)S(1)} %copy-done), channel_id=1, source_target_pairs={{8,16},{12,20},{16,8},{20,12},{9,17},{13,21},{17,9},{21,13},{10,18... | collective-permute-start | bytes 294920 | tf_op jit(solution)/shard_map/ppermute | solution.py:290
  17.5 2.0 %attention.1 = (bf16[128,384]{1,0:T(8,128)(2,1)S(1)}, f32[128,128]{1,0:T(8,128)S(1)}, f32[8,128]{1,0:T(8,128)S(1)}) custom-call(s32[1,4]{1,0:T(1,128)S(1)} %copy-done.2, bf16[128,384]{1,0:T(8,128)(2,1)S(1)} %copy-done, bf16[128,384]{1,0:T(8,128)(2,1)S(1)} %copy-done.1, f32[1,384]{1,0:T(1,128)S(1)} %broadcast_in_dim.3.gain_ref.refs_3_, ...), custom_call_target="tpu_custom_call" | custom-call | tf_op jit(solution)/shard_map/attention/pallas_call | solution.py:243
  19.5 1.3 %collective-permute-start.7 = (f32[8,128]{1,0:T(8,128)S(1)}, f32[8,128]{1,0:T(8,128)S(1)}, u32[]{:S(2)}, u32[]{:S(2)}) collective-permute-start(f32[8,128]{1,0:T(8,128)S(1)} %get-tuple-element.28.refs_4_), channel_id=1, source_target_pairs={{0,1},{1,0},{2,3},{3,2},{4,5},{5,4},{6,7},{7,6},{8,9},{9,8},{10,11... | collective-permute-start | bytes 12296 | tf_op jit(solution)/shard_map/ppermute | solution.py:273
  20.8 2.3 %collective-permute-start.8 = (f32[8,128]{1,0:T(8,128)S(1)}, f32[8,128]{1,0:T(8,128)S(1)}, u32[]{:S(2)}, u32[]{:S(2)}) collective-permute-start(f32[8,128]{1,0:T(8,128)S(1)} %get-tuple-element.28.refs_4_), channel_id=1, source_target_pairs={{0,2},{1,3},{2,0},{3,1},{4,6},{5,7},{6,4},{7,5},{8,10},{9,11},{10,... | collective-permute-start | bytes 12296 | tf_op jit(solution)/shard_map/ppermute | solution.py:273
  23.2 1.0 %collective-permute-done.8.refs_6_ = f32[8,128]{1,0:T(8,128)S(1)} collective-permute-done((f32[8,128]{1,0:T(8,128)S(1)}, f32[8,128]{1,0:T(8,128)S(1)}, u32[]{:S(2)}, u32[]{:S(2)}) %collective-permute-start.8) | collective-permute-done | bytes 4128 | tf_op jit(solution)/shard_map/ppermute | solution.py:273
  24.2 3.2 %collective-permute-done.9.refs_7_ = f32[8,128]{1,0:T(8,128)S(1)} collective-permute-done((f32[8,128]{1,0:T(8,128)S(1)}, f32[8,128]{1,0:T(8,128)S(1)}, u32[]{:S(2)}, u32[]{:S(2)}) %collective-permute-start.9) | collective-permute-done | bytes 4128 | tf_op jit(solution)/shard_map/ppermute | solution.py:273
  27.4 0.9 %attention_gradient.1 = (bf16[144,384]{1,0:T(8,128)(2,1)S(1)}, f32[128,128]{1,0:T(8,128)S(1)}) custom-call(s32[1,4]{1,0:T(1,128)S(1)} %copy-done.2, bf16[128,384]{1,0:T(8,128)(2,1)S(1)} %get-tuple-element.26.refs_1_.attn_ref, bf16[128,384]{1,0:T(8,128)(2,1)S(1)} %copy-done.1, f32[1,384]{1,0:T(1,128)S(1)} %broadcast_in_dim.3.gain_ref.refs_3_, ...), custom_call_target="tpu_custom_call" | custom-call | tf_op jit(solution)/shard_map/attention_gradient/pallas_call | solution.py:243
  28.3 2.5 %collective-permute-start.10 = (bf16[144,384]{1,0:T(8,128)(2,1)S(1)}, bf16[144,384]{1,0:T(8,128)(2,1)S(1)}, u32[]{:S(2)}, u32[]{:S(2)}) collective-permute-start(bf16[144,384]{1,0:T(8,128)(2,1)S(1)} %get-tuple-element.42.msg_ref.m0), channel_id=1, source_target_pairs={{0,4},{4,0},{8,12},{12,8},{16,20},{20,16},{24,28},{28,24},{1,5},{5... | collective-permute-start | bytes 331784 | tf_op jit(solution)/shard_map/ppermute | solution.py:292
  30.8 2.1 %collective-permute-start.12 = (bf16[144,384]{1,0:T(8,128)(2,1)S(1)}, bf16[144,384]{1,0:T(8,128)(2,1)S(1)}, u32[]{:S(2)}, u32[]{:S(2)}) collective-permute-start(bf16[144,384]{1,0:T(8,128)(2,1)S(1)} %get-tuple-element.42.msg_ref.m0), channel_id=1, source_target_pairs={{8,16},{12,20},{16,8},{20,12},{9,17},{13,21},{17,9},{21,13},{10,18... | collective-permute-start | bytes 331784 | tf_op jit(solution)/shard_map/ppermute | solution.py:290
  32.9 2.1 %query_gradient.1 = (bf16[128,384]{1,0:T(8,128)(2,1)}, bf16[128,384]{1,0:T(8,128)(2,1)}) custom-call(s32[1,4]{1,0:T(1,128)S(1)} %copy-done.2, bf16[128,384]{1,0:T(8,128)(2,1)S(1)} %copy-done, f32[1,384]{1,0:T(1,128)S(1)} %broadcast_in_dim.3.gain_ref.refs_3_, bf16[128,384]{1,0:T(8,128)(2,1)S(1)} %get-tuple-element.26.refs_1_.attn_ref, ...), custom_call_target="tpu_custom_call" | custom-call | tf_op jit(solution)/shard_map/query_gradient/pallas_call | solution.py:243
  35.0 0.4 collective-permute-done.11.m2
  35.4 2.8 %collective-permute-done.12.m3 = bf16[144,384]{1,0:T(8,128)(2,1)S(1)} collective-permute-done((bf16[144,384]{1,0:T(8,128)(2,1)S(1)}, bf16[144,384]{1,0:T(8,128)(2,1)S(1)}, u32[]{:S(2)}, u32[]{:S(2)}) %collective-permute-start.12) | collective-permute-done | bytes 110624 | tf_op jit(solution)/shard_map/ppermute | solution.py:290
  38.2 0.9 %collective-permute-start.14 = (bf16[144,384]{1,0:T(8,128)(2,1)S(1)}, bf16[144,384]{1,0:T(8,128)(2,1)S(1)}, u32[]{:S(2)}, u32[]{:S(2)}) collective-permute-start(bf16[144,384]{1,0:T(8,128)(2,1)S(1)} %broadcast_select_fusion.1), channel_id=1, source_target_pairs={{0,4},{4,0},{8,12},{12,8},{16,20},{20,16},{24,28},{28,24},{1,5},{5... | collective-permute-start | bytes 331784 | tf_op jit(solution)/shard_map/ppermute | solution.py:296
  39.2 0.1 collective-permute-start.13
  39.3 1.3 %collective-permute-done.13.q4 = bf16[128,384]{1,0:T(8,128)(2,1)S(1)} collective-permute-done((bf16[128,384]{1,0:T(8,128)(2,1)S(1)}, bf16[128,384]{1,0:T(8,128)(2,1)S(1)}, u32[]{:S(2)}, u32[]{:S(2)}) %collective-permute-start.13) | collective-permute-done | bytes 98336 | tf_op jit(solution)/shard_map/ppermute | solution.py:296
  40.5 1.6 %key_gradient.1 = (bf16[128,384]{1,0:T(8,128)(2,1)}, bf16[128,384]{1,0:T(8,128)(2,1)}) custom-call(bf16[2,128,384]{2,1,0:T(8,128)(2,1)S(1)} %pad_maximum_fusion.own, bf16[128,384]{1,0:T(8,128)(2,1)S(1)} %copy-done, bf16[128,384]{1,0:T(8,128)(2,1)S(1)} %collective-permute-done.4.q1, bf16[128,384]{1,0:T(8,128)(2,1)S(1)} %collective-permute-done.5.q2, ...), custom_call_target="tpu_custom_call" | custom-call | tf_op jit(solution)/shard_map/key_gradient/pallas_call | solution.py:243
  (23 shorter events, 0.1 us)
Async XLA Ops:
  1.6 5.8 %collective-permute-start.1 = (bf16[2,128,384]{2,1,0:T(8,128)(2,1)S(1)}, bf16[2,128,384]{2,1,0:T(8,128)(2,1)S(1)}, u32[]{:S(2)}, u32[]{:S(2)}) collective-permute-start(bf16[2,128,384]{2,1,0:T(8,128)(2,1)S(1)} %pad_maximum_fusion.own), channel_id=1, source_target_pairs={{0,8},{4,12},{8,0},{12,4},{16,24},{20,28},{24,16},{28,20},{1,9},{5... | collective-permute-start | bytes 589832 | tf_op jit(solution)/shard_map/ppermute | solution.py:291
  2.9 8.2 %collective-permute-start.2 = (bf16[2,128,384]{2,1,0:T(8,128)(2,1)S(1)}, bf16[2,128,384]{2,1,0:T(8,128)(2,1)S(1)}, u32[]{:S(2)}, u32[]{:S(2)}) collective-permute-start(bf16[2,128,384]{2,1,0:T(8,128)(2,1)S(1)} %pad_maximum_fusion.own), channel_id=1, source_target_pairs={{8,16},{12,20},{16,8},{20,12},{9,17},{13,21},{17,9},{21,13},{10,18... | collective-permute-start | bytes 589832 | tf_op jit(solution)/shard_map/ppermute | solution.py:290
  4.8 12.6 %collective-permute-start = (bf16[2,128,384]{2,1,0:T(8,128)(2,1)S(1)}, bf16[2,128,384]{2,1,0:T(8,128)(2,1)S(1)}, u32[]{:S(2)}, u32[]{:S(2)}) collective-permute-start(bf16[2,128,384]{2,1,0:T(8,128)(2,1)S(1)} %pad_maximum_fusion.own), channel_id=1, source_target_pairs={{0,4},{4,0},{8,12},{12,8},{16,20},{20,16},{24,28},{28,24},{1,5},{5... | collective-permute-start | bytes 589832 | tf_op jit(solution)/shard_map/ppermute | solution.py:292
  5.8 7.3 %copy-start = (bf16[128,384]{1,0:T(8,128)(2,1)S(1)}, bf16[128,384]{1,0:T(8,128)(2,1)}, u32[]{:S(2)}) copy-start(bf16[128,384]{1,0:T(8,128)(2,1)} %q0) | copy-start | bytes 294916
  5.8 11.6 %copy-start.3 = (f32[384]{0:T(512)S(1)}, f32[384]{0:T(512)}, u32[]{:S(2)}) copy-start(f32[384]{0:T(512)} %param.10) | copy-start | bytes 4612
  5.8 11.6 %copy-start.1 = (bf16[128,384]{1,0:T(8,128)(2,1)S(1)}, bf16[128,384]{1,0:T(8,128)(2,1)}, u32[]{:S(2)}) copy-start(bf16[128,384]{1,0:T(8,128)(2,1)} %refs_2_.1) | copy-start | bytes 294916
  11.1 6.3 %copy-start.2 = (s32[1,4]{1,0:T(1,128)S(1)}, s32[1,4]{1,0:T(1,128)}, u32[]{:S(2)}) copy-start(s32[1,4]{1,0:T(1,128)} %flags_ref.3) | copy-start | bytes 52
  11.2 6.3 %collective-permute-start.3 = (bf16[2,128,384]{2,1,0:T(8,128)(2,1)S(1)}, bf16[2,128,384]{2,1,0:T(8,128)(2,1)S(1)}, u32[]{:S(2)}, u32[]{:S(2)}) collective-permute-start(bf16[2,128,384]{2,1,0:T(8,128)(2,1)S(1)} %broadcast_select_fusion), channel_id=1, source_target_pairs={{0,4},{4,0},{8,12},{12,8},{16,20},{20,16},{24,28},{28,24},{1,5},{5... | collective-permute-start | bytes 589832 | tf_op jit(solution)/shard_map/ppermute | solution.py:296
  13.1 10.1 %collective-permute-start.4 = (bf16[128,384]{1,0:T(8,128)(2,1)S(1)}, bf16[128,384]{1,0:T(8,128)(2,1)S(1)}, u32[]{:S(2)}, u32[]{:S(2)}) collective-permute-start(bf16[128,384]{1,0:T(8,128)(2,1)S(1)} %copy-done), channel_id=1, source_target_pairs={{0,4},{4,0},{8,12},{12,8},{16,20},{20,16},{24,28},{28,24},{1,5},{5... | collective-permute-start | bytes 294920 | tf_op jit(solution)/shard_map/ppermute | solution.py:292
  13.2 10.0 %collective-permute-start.5 = (bf16[128,384]{1,0:T(8,128)(2,1)S(1)}, bf16[128,384]{1,0:T(8,128)(2,1)S(1)}, u32[]{:S(2)}, u32[]{:S(2)}) collective-permute-start(bf16[128,384]{1,0:T(8,128)(2,1)S(1)} %copy-done), channel_id=1, source_target_pairs={{0,8},{4,12},{8,0},{12,4},{16,24},{20,28},{24,16},{28,20},{1,9},{5... | collective-permute-start | bytes 294920 | tf_op jit(solution)/shard_map/ppermute | solution.py:291
  13.2 10.0 %collective-permute-start.6 = (bf16[128,384]{1,0:T(8,128)(2,1)S(1)}, bf16[128,384]{1,0:T(8,128)(2,1)S(1)}, u32[]{:S(2)}, u32[]{:S(2)}) collective-permute-start(bf16[128,384]{1,0:T(8,128)(2,1)S(1)} %copy-done), channel_id=1, source_target_pairs={{8,16},{12,20},{16,8},{20,12},{9,17},{13,21},{17,9},{21,13},{10,18... | collective-permute-start | bytes 294920 | tf_op jit(solution)/shard_map/ppermute | solution.py:290
  19.5 3.7 %collective-permute-start.7 = (f32[8,128]{1,0:T(8,128)S(1)}, f32[8,128]{1,0:T(8,128)S(1)}, u32[]{:S(2)}, u32[]{:S(2)}) collective-permute-start(f32[8,128]{1,0:T(8,128)S(1)} %get-tuple-element.28.refs_4_), channel_id=1, source_target_pairs={{0,1},{1,0},{2,3},{3,2},{4,5},{5,4},{6,7},{7,6},{8,9},{9,8},{10,11... | collective-permute-start | bytes 12296 | tf_op jit(solution)/shard_map/ppermute | solution.py:273
  20.8 3.4 %collective-permute-start.8 = (f32[8,128]{1,0:T(8,128)S(1)}, f32[8,128]{1,0:T(8,128)S(1)}, u32[]{:S(2)}, u32[]{:S(2)}) collective-permute-start(f32[8,128]{1,0:T(8,128)S(1)} %get-tuple-element.28.refs_4_), channel_id=1, source_target_pairs={{0,2},{1,3},{2,0},{3,1},{4,6},{5,7},{6,4},{7,5},{8,10},{9,11},{10,... | collective-permute-start | bytes 12296 | tf_op jit(solution)/shard_map/ppermute | solution.py:273
  23.2 4.3 %collective-permute-start.9 = (f32[8,128]{1,0:T(8,128)S(1)}, f32[8,128]{1,0:T(8,128)S(1)}, u32[]{:S(2)}, u32[]{:S(2)}) collective-permute-start(f32[8,128]{1,0:T(8,128)S(1)} %get-tuple-element.28.refs_4_), channel_id=1, source_target_pairs={{0,3},{1,2},{2,1},{3,0},{4,7},{5,6},{6,5},{7,4},{8,11},{9,10},{10,... | collective-permute-start | bytes 12296 | tf_op jit(solution)/shard_map/ppermute | solution.py:273
  28.3 6.7 %collective-permute-start.10 = (bf16[144,384]{1,0:T(8,128)(2,1)S(1)}, bf16[144,384]{1,0:T(8,128)(2,1)S(1)}, u32[]{:S(2)}, u32[]{:S(2)}) collective-permute-start(bf16[144,384]{1,0:T(8,128)(2,1)S(1)} %get-tuple-element.42.msg_ref.m0), channel_id=1, source_target_pairs={{0,4},{4,0},{8,12},{12,8},{16,20},{20,16},{24,28},{28,24},{1,5},{5... | collective-permute-start | bytes 331784 | tf_op jit(solution)/shard_map/ppermute | solution.py:292
  30.8 4.6 %collective-permute-start.11 = (bf16[144,384]{1,0:T(8,128)(2,1)S(1)}, bf16[144,384]{1,0:T(8,128)(2,1)S(1)}, u32[]{:S(2)}, u32[]{:S(2)}) collective-permute-start(bf16[144,384]{1,0:T(8,128)(2,1)S(1)} %get-tuple-element.42.msg_ref.m0), channel_id=1, source_target_pairs={{0,8},{4,12},{8,0},{12,4},{16,24},{20,28},{24,16},{28,20},{1,9},{5... | collective-permute-start | bytes 331784 | tf_op jit(solution)/shard_map/ppermute | solution.py:291
  30.8 7.4 %collective-permute-start.12 = (bf16[144,384]{1,0:T(8,128)(2,1)S(1)}, bf16[144,384]{1,0:T(8,128)(2,1)S(1)}, u32[]{:S(2)}, u32[]{:S(2)}) collective-permute-start(bf16[144,384]{1,0:T(8,128)(2,1)S(1)} %get-tuple-element.42.msg_ref.m0), channel_id=1, source_target_pairs={{8,16},{12,20},{16,8},{20,12},{9,17},{13,21},{17,9},{21,13},{10,18... | collective-permute-start | bytes 331784 | tf_op jit(solution)/shard_map/ppermute | solution.py:290
  38.2 2.3 %collective-permute-start.14 = (bf16[144,384]{1,0:T(8,128)(2,1)S(1)}, bf16[144,384]{1,0:T(8,128)(2,1)S(1)}, u32[]{:S(2)}, u32[]{:S(2)}) collective-permute-start(bf16[144,384]{1,0:T(8,128)(2,1)S(1)} %broadcast_select_fusion.1), channel_id=1, source_target_pairs={{0,4},{4,0},{8,12},{12,8},{16,20},{20,16},{24,28},{28,24},{1,5},{5... | collective-permute-start | bytes 331784 | tf_op jit(solution)/shard_map/ppermute | solution.py:296
  39.2 1.4 %collective-permute-start.13 = (bf16[128,384]{1,0:T(8,128)(2,1)S(1)}, bf16[128,384]{1,0:T(8,128)(2,1)S(1)}, u32[]{:S(2)}, u32[]{:S(2)}) collective-permute-start(bf16[128,384]{1,0:T(8,128)(2,1)S(1)} %broadcast_select_fusion.2), channel_id=1, source_target_pairs={{0,4},{4,0},{8,12},{12,8},{16,20},{20,16},{24,28},{28,24},{1,5},{5... | collective-permute-start | bytes 294920 | tf_op jit(solution)/shard_map/ppermute | solution.py:296
where the time goes:
time: 42.3 us; the launch traced here: 42.1 us
  starting transfers between devices  19.7 us (47%)
  waiting for transfers between devices  14 us (33%)
  Pallas kernels  6.59 us (16%)
  other arithmetic  1.03 us (2%)
  between operations  0.76 us (2%)
    ppermute x3, starting transfers between devices, swaps(): outer = lax.ppermute(array, 'band', outer_pairs)  8.27 us
    pallas_call x4, Pallas kernels, call(): pl.pallas_call(kernel, name=name, out_shape=out_shape, in_specs=specs, ou...  6.59 us
    ppermute x3, waiting for transfers between devices, swaps(): outer = lax.ppermute(array, 'band', outer_pairs)  6.44 us
    ppermute x3, waiting for transfers between devices, head_sum_parts(): parts.append(lax.ppermute(stats, 'head', pairs))  4.23 us
    ppermute x3, starting transfers between devices, head_sum_parts(): parts.append(lax.ppermute(stats, 'head', pairs))  3.65 us
    ppermute x3, starting transfers between devices, swaps(): return (array, lax.ppermute(array, 'band', partner_pairs), inner, outer)  3.58 us
    ppermute x3, starting transfers between devices, with_fifth(): return tuple(held) + (lax.ppermute(passed, 'band', partner_pairs),)  2.95 us
    ppermute x3, waiting for transfers between devices, swaps(): inner = lax.ppermute(array, 'band', inner_pairs)  2.03 us
  transfers between devices with their start and end apart: 15, of which 7 were waited for; matrix products, arithmetic and copies ran while one was open for 0% of the time, Pallas kernels for 10%

commit v1 on v0

--- a/solution.py
+++ b/solution.py
@@ -63,9 +63,9 @@
     first, even = is_even(spacing)
     return [
         None,
+        jnp.where(even, m2, p2) == 1,
+        jnp.where(even, p2, m2) == 1,
         jnp.where(first, p1, m1) == 1,
-        jnp.where(even, p2, m2) == 1,
-        jnp.where(even, m2, p2) == 1,
         jnp.where(first, m1, p1) == 1,
     ]
 
@@ -82,13 +82,13 @@
 
 
 def forward_kernel(
-    spacing, blocks, flags_ref, q_ref, g_ref, gain_ref, own, partner, inner, outer, fifth,
+    spacing, blocks, flags_ref, q_ref, g_ref, gain_ref, own, outer, inner, partner, fifth,
     attn_ref, cols_ref, stats_ref,
 ):
     rows = q_ref.shape[0]
     heads = q_ref.shape[1] // HEAD_DIM
     flags = slot_flags(flags_ref, spacing, blocks)
-    held = [own, partner, inner, outer, fifth]
+    held = [own, outer, inner, partner, fifth]
     square = jnp.zeros((rows, HEAD_DIM), F32)
     along = jnp.zeros((rows, HEAD_DIM), F32)
     peaks, inverse_totals = [], []
@@ -120,19 +120,16 @@
         rows,
     )
     cols_ref[...] = cols
-    stats_ref[...] = cols.T[: stats_ref.shape[0]]
+    stats_ref[...] = jnp.broadcast_to(cols.T[None, : stats_ref.shape[1]], stats_ref.shape)
 
 
 def message_kernel(
-    width, n_parts, *refs
+    width, flags_ref, attn_ref, g_ref, gain_ref, stats_ref, parts_ref, msg_ref, cols_ref
 ):
-    flags_ref, attn_ref, g_ref, gain_ref = refs[:4]
-    part_refs = refs[4 : 4 + n_parts]
-    msg_ref, cols_ref = refs[4 + n_parts :]
     rows = attn_ref.shape[0]
     heads = attn_ref.shape[1] // HEAD_DIM
-    own = part_refs[0][...]
-    total = functools.reduce(jnp.add, [r[...] for r in part_refs])
+    own = stats_ref[0]
+    total = jnp.sum(parts_ref[...], axis=0)
     square = total[2 * heads : 2 * heads + 1]
     along = total[2 * heads + 1 : 2 * heads + 2]
     inverse = lax.rsqrt(square / width + EPS)
@@ -171,12 +168,12 @@
 
 def query_kernel(
     spacing, blocks, flags_ref, q_ref, gain_ref, attn_ref, msg_ref, cols_ref, cols2_ref,
-    own, partner, inner, outer, fifth, out_ref, dq_ref,
+    own, outer, inner, partner, fifth, out_ref, dq_ref,
 ):
     rows = q_ref.shape[0]
     heads = q_ref.shape[1] // HEAD_DIM
     flags = slot_flags(flags_ref, spacing, blocks)
-    held = [own, partner, inner, outer, fifth]
+    held = [own, outer, inner, partner, fifth]
     inverse = cols2_ref[:, heads : heads + 1]
     for h in range(heads):
         sl = head_slice(h)
@@ -221,9 +218,9 @@
                 at_m2, at_m1, at_p1, at_p2 = [stats[9 + i : 10 + i] for i in range(4)]
                 flag = [
                     None,
+                    jnp.where(even, at_p2, at_m2),
+                    jnp.where(even, at_m2, at_p2),
                     jnp.where(first, at_m1, at_p1),
-                    jnp.where(even, at_m2, at_p2),
-                    jnp.where(even, at_p2, at_m2),
                     jnp.where(first, at_p1, at_m1),
                 ][j]
                 score = jnp.where(flag > 0.5, score, NEG)
@@ -263,17 +260,6 @@
     return partner, inner, outer
 
 
-def head_sum_parts(stats, devices):
-    parts = [stats]
-    for k in range(1, devices):
-        if devices & (devices - 1) == 0:
-            pairs = [(i, i ^ k) for i in range(devices)]
-        else:
-            pairs = [(i, (i + k) % devices) for i in range(devices)]
-        parts.append(lax.ppermute(stats, "head", pairs))
-    return parts
-
-
 def local(queries, keys, values, d_out, gain, blocks_on):
     rows, width_here = queries.shape
     blocks = lax.axis_size("band")
@@ -287,12 +273,13 @@
     first, even = is_even(spacing)
 
     def swaps(array):
-        outer = lax.ppermute(array, "band", outer_pairs)
-        inner = lax.ppermute(array, "band", inner_pairs)
-        return array, lax.ppermute(array, "band", partner_pairs), inner, outer
+        return (array,) + tuple(
+            lax.ppermute(array, "band", pairs)
+            for pairs in (outer_pairs, inner_pairs, partner_pairs)
+        )
 
     def with_fifth(held):
-        passed = lax.select(first == even, held[2], held[3])
+        passed = lax.select(first == even, held[2], held[1])
         return tuple(held) + (lax.ppermute(passed, "band", partner_pairs),)
 
     kv = swaps(jnp.stack([keys, values]))
@@ -305,18 +292,17 @@
         (
             shape((rows, width_here), BF16),
             shape((rows, HEAD_DIM), F32),
-            shape((2 * heads + 2, HEAD_DIM), F32),
+            shape((head_devices, 2 * heads + 2, HEAD_DIM), F32),
         ),
         (blocks_on, queries, d_out, gain) + kv,
     )
-    parts = head_sum_parts(stats, head_devices)
+    parts = lax.all_to_all(stats, "head", 0, 0)
     qs, parts = lax.optimization_barrier((qs, parts))
-    qs = with_fifth(qs)
     msg, cols2 = call(
-        functools.partial(message_kernel, width, head_devices),
+        functools.partial(message_kernel, width),
         "attention_gradient",
         (shape((rows + STAT_ROWS, width_here), BF16), shape((rows, HEAD_DIM), F32)),
-        (blocks_on, attn, d_out, gain) + tuple(parts),
+        (blocks_on, attn, d_out, gain, stats, parts),
     )
     msgs = swaps(msg)
     out, d_queries = call(
@@ -325,7 +311,8 @@
         (shape((rows, width_here), BF16),) * 2,
         (blocks_on, queries, gain, attn, msg, cols, cols2) + kv,
     )
-    msgs, d_queries = lax.optimization_barrier((msgs, d_queries))
+    qs = with_fifth(qs)
+    msgs, d_queries, qs = lax.optimization_barrier((msgs, d_queries, qs))
     msgs = with_fifth(msgs)
     d_keys, d_values = call(
         functools.partial(key_kernel, spacing),

time: 42.3 us -> 45.2 us (1.069)
  the two profiles are of different devices: /device:TPU:5 before, /device:TPU:0 now
where the time goes in v1:
time: 45.2 us; the launch traced here: 44.9 us
  starting transfers between devices  18.7 us (41%)
  waiting for transfers between devices  17.1 us (38%)
  Pallas kernels  7.36 us (16%)
  other arithmetic  1.03 us (2%)
  between operations  0.77 us (2%)
    ppermute x9, starting transfers between devices, swaps(): lax.ppermute(array, 'band', pairs)  13.1 us
    ppermute x9, waiting for transfers between devices, swaps(): lax.ppermute(array, 'band', pairs)  10.2 us
    pallas_call x4, Pallas kernels, call(): pl.pallas_call(kernel, name=name, out_shape=out_shape, in_specs=specs, ou...  7.36 us
    all_to_all x1, waiting for transfers between devices, local(): parts = lax.all_to_all(stats, 'head', 0, 0)  5.59 us
    all_to_all x1, starting transfers between devices, local(): parts = lax.all_to_all(stats, 'head', 0, 0)  4.87 us
    ppermute x3, waiting for transfers between devices, with_fifth(): return tuple(held) + (lax.ppermute(passed, 'band', partner_pairs),)  1.31 us
    another operation x1, other arithmetic, local(): kv = swaps(jnp.stack([keys, values]))  0.97 us
  transfers between devices with their start and end apart: 13, of which 4 were waited for; matrix products, arithmetic and copies ran while one was open for 0% of the time, Pallas kernels for 10%

profile of v1, /device:TPU:0, one launch (start us, length us, event | category | flops | bytes accessed | tf_op | source)
XLA Modules:
  0.0 44.9 jit_solution(17669995470995414019)
XLA Ops:
  0.6 1.0 %pad_maximum_fusion.own = bf16[2,128,384]{2,1,0:T(8,128)(2,1)S(1)} fusion(bf16[1,128,384]{2,1,0:T(8,128)(2,1)} %bitcast.2, bf16[1,128,384]{2,1,0:T(8,128)(2,1)} %bitcast.3), kind=kLoop, calls=%fused_computation | loop fusion | flops 98304 | bytes 393216 | tf_op jit(solution)/shard_map/stack | solution.py:285
  1.6 0.7 %collective-permute-start = (bf16[2,128,384]{2,1,0:T(8,128)(2,1)S(1)}, bf16[2,128,384]{2,1,0:T(8,128)(2,1)S(1)}, u32[]{:S(2)}, u32[]{:S(2)}) collective-permute-start(bf16[2,128,384]{2,1,0:T(8,128)(2,1)S(1)} %pad_maximum_fusion.own), channel_id=1, source_target_pairs={{8,16},{12,20},{16,8},{20,12},{9,17},{13,21},{17,9},{21,13},{10,18... | collective-permute-start | bytes 589832 | tf_op jit(solution)/shard_map/ppermute | solution.py:277
  2.3 5.7 %collective-permute-start.1 = (bf16[2,128,384]{2,1,0:T(8,128)(2,1)S(1)}, bf16[2,128,384]{2,1,0:T(8,128)(2,1)S(1)}, u32[]{:S(2)}, u32[]{:S(2)}) collective-permute-start(bf16[2,128,384]{2,1,0:T(8,128)(2,1)S(1)} %pad_maximum_fusion.own), channel_id=1, source_target_pairs={{0,8},{4,12},{8,0},{12,4},{16,24},{20,28},{24,16},{28,20},{1,9},{5... | collective-permute-start | bytes 589832 | tf_op jit(solution)/shard_map/ppermute | solution.py:277
  8.0 0.0 collective-permute-start.2
  8.0 0.0 collective-permute-done.outer
  8.0 8.7 %collective-permute-done.1.inner = bf16[2,128,384]{2,1,0:T(8,128)(2,1)S(1)} collective-permute-done((bf16[2,128,384]{2,1,0:T(8,128)(2,1)S(1)}, bf16[2,128,384]{2,1,0:T(8,128)(2,1)S(1)}, u32[]{:S(2)}, u32[]{:S(2)}) %collective-permute-start.1) | collective-permute-done | bytes 196640 | tf_op jit(solution)/shard_map/ppermute | solution.py:277
  16.8 0.0 copy-start.2
  16.8 0.1 collective-permute-start.3
  16.9 0.7 %collective-permute-start.4 = (bf16[128,384]{1,0:T(8,128)(2,1)S(1)}, bf16[128,384]{1,0:T(8,128)(2,1)S(1)}, u32[]{:S(2)}, u32[]{:S(2)}) collective-permute-start(bf16[128,384]{1,0:T(8,128)(2,1)S(1)} %copy-done), channel_id=1, source_target_pairs={{8,16},{12,20},{16,8},{20,12},{9,17},{13,21},{17,9},{21,13},{10,18... | collective-permute-start | bytes 294920 | tf_op jit(solution)/shard_map/ppermute | solution.py:277
  17.6 2.3 %collective-permute-start.5 = (bf16[128,384]{1,0:T(8,128)(2,1)S(1)}, bf16[128,384]{1,0:T(8,128)(2,1)S(1)}, u32[]{:S(2)}, u32[]{:S(2)}) collective-permute-start(bf16[128,384]{1,0:T(8,128)(2,1)S(1)} %copy-done), channel_id=1, source_target_pairs={{0,8},{4,12},{8,0},{12,4},{16,24},{20,28},{24,16},{28,20},{1,9},{5... | collective-permute-start | bytes 294920 | tf_op jit(solution)/shard_map/ppermute | solution.py:277
  19.8 0.0 collective-permute-start.6
  19.9 0.0 collective-permute-done.3.fifth
  19.9 2.6 %attention.1 = (bf16[128,384]{1,0:T(8,128)(2,1)S(1)}, f32[128,128]{1,0:T(8,128)S(1)}, f32[4,8,128]{2,1,0:T(8,128)}) custom-call(s32[1,4]{1,0:T(1,128)S(1)} %copy-done.2, bf16[128,384]{1,0:T(8,128)(2,1)S(1)} %copy-done, bf16[128,384]{1,0:T(8,128)(2,1)S(1)} %copy-done.1, f32[1,384]{1,0:T(1,128)S(1)} %broadcast_in_dim.3.gain_ref, ...), custom_call_target="tpu_custom_call" | custom-call | tf_op jit(solution)/shard_map/attention/pallas_call | solution.py:240
  22.5 4.9 %all-to-all-start = ((f32[4,8,128]{2,1,0:T(8,128)}), f32[4,8,128]{2,1,0:T(8,128)S(1)}, u32[]{:S(2)}, u32[]{:S(2)}) async-start(f32[4,8,128]{2,1,0:T(8,128)} %get-tuple-element.29.stats_ref), calls=%async_computation | async-start | bytes 32768 | tf_op jit(solution)/shard_map/all_to_all | solution.py:299
  27.4 5.6 %all-to-all-done.parts_ref = f32[4,8,128]{2,1,0:T(8,128)S(1)} async-done(((f32[4,8,128]{2,1,0:T(8,128)}), f32[4,8,128]{2,1,0:T(8,128)S(1)}, u32[]{:S(2)}, u32[]{:S(2)}) %all-to-all-start) | async-done | bytes 16416 | tf_op jit(solution)/shard_map/all_to_all | solution.py:299
  33.0 1.1 %attention_gradient.1 = (bf16[144,384]{1,0:T(8,128)(2,1)S(1)}, f32[128,128]{1,0:T(8,128)S(1)}) custom-call(s32[1,4]{1,0:T(1,128)S(1)} %copy-done.2, bf16[128,384]{1,0:T(8,128)(2,1)S(1)} %get-tuple-element.28.attn_ref, bf16[128,384]{1,0:T(8,128)(2,1)S(1)} %copy-done.1, f32[1,384]{1,0:T(1,128)S(1)} %broadcast_in_dim.3.gain_ref, ...), custom_call_target="tpu_custom_call" | custom-call | tf_op jit(solution)/shard_map/attention_gradient/pallas_call | solution.py:240
  34.1 0.7 %collective-permute-start.7 = (bf16[144,384]{1,0:T(8,128)(2,1)S(1)}, bf16[144,384]{1,0:T(8,128)(2,1)S(1)}, u32[]{:S(2)}, u32[]{:S(2)}) collective-permute-start(bf16[144,384]{1,0:T(8,128)(2,1)S(1)} %get-tuple-element.46.msg_ref.m0), channel_id=1, source_target_pairs={{8,16},{12,20},{16,8},{20,12},{9,17},{13,21},{17,9},{21,13},{10,18... | collective-permute-start | bytes 331784 | tf_op jit(solution)/shard_map/ppermute | solution.py:277
  34.8 3.1 %collective-permute-start.8 = (bf16[144,384]{1,0:T(8,128)(2,1)S(1)}, bf16[144,384]{1,0:T(8,128)(2,1)S(1)}, u32[]{:S(2)}, u32[]{:S(2)}) collective-permute-start(bf16[144,384]{1,0:T(8,128)(2,1)S(1)} %get-tuple-element.46.msg_ref.m0), channel_id=1, source_target_pairs={{0,8},{4,12},{8,0},{12,4},{16,24},{20,28},{24,16},{28,20},{1,9},{5... | collective-permute-start | bytes 331784 | tf_op jit(solution)/shard_map/ppermute | solution.py:277
  37.9 0.6 %collective-permute-start.10 = (bf16[128,384]{1,0:T(8,128)(2,1)S(1)}, bf16[128,384]{1,0:T(8,128)(2,1)S(1)}, u32[]{:S(2)}, u32[]{:S(2)}) collective-permute-start(bf16[128,384]{1,0:T(8,128)(2,1)S(1)} %broadcast_select_fusion.2), channel_id=1, source_target_pairs={{0,4},{4,0},{8,12},{12,8},{16,20},{20,16},{24,28},{28,24},{1,5},{5... | collective-permute-start | bytes 294920 | tf_op jit(solution)/shard_map/ppermute | solution.py:283
  38.4 2.1 %query_gradient.1 = (bf16[128,384]{1,0:T(8,128)(2,1)}, bf16[128,384]{1,0:T(8,128)(2,1)}) custom-call(s32[1,4]{1,0:T(1,128)S(1)} %copy-done.2, bf16[128,384]{1,0:T(8,128)(2,1)S(1)} %copy-done, f32[1,384]{1,0:T(1,128)S(1)} %broadcast_in_dim.3.gain_ref, bf16[128,384]{1,0:T(8,128)(2,1)S(1)} %get-tuple-element.28.attn_ref, ...), custom_call_target="tpu_custom_call" | custom-call | tf_op jit(solution)/shard_map/query_gradient/pallas_call | solution.py:240
  40.5 1.4 %collective-permute-done.8.m2 = bf16[144,384]{1,0:T(8,128)(2,1)S(1)} collective-permute-done((bf16[144,384]{1,0:T(8,128)(2,1)S(1)}, bf16[144,384]{1,0:T(8,128)(2,1)S(1)}, u32[]{:S(2)}, u32[]{:S(2)}) %collective-permute-start.8) | collective-permute-done | bytes 110624 | tf_op jit(solution)/shard_map/ppermute | solution.py:277
  42.0 0.1 collective-permute-start.11
  42.1 1.3 %collective-permute-done.11.m4 = bf16[144,384]{1,0:T(8,128)(2,1)S(1)} collective-permute-done((bf16[144,384]{1,0:T(8,128)(2,1)S(1)}, bf16[144,384]{1,0:T(8,128)(2,1)S(1)}, u32[]{:S(2)}, u32[]{:S(2)}) %collective-permute-start.11) | collective-permute-done | bytes 110624 | tf_op jit(solution)/shard_map/ppermute | solution.py:283
  43.4 1.6 %key_gradient.1 = (bf16[128,384]{1,0:T(8,128)(2,1)}, bf16[128,384]{1,0:T(8,128)(2,1)}) custom-call(bf16[2,128,384]{2,1,0:T(8,128)(2,1)S(1)} %pad_maximum_fusion.own, bf16[128,384]{1,0:T(8,128)(2,1)S(1)} %copy-done, bf16[128,384]{1,0:T(8,128)(2,1)S(1)} %collective-permute-done.4.q1, bf16[128,384]{1,0:T(8,128)(2,1)S(1)} %collective-permute-done.5.q2, ...), custom_call_target="tpu_custom_call" | custom-call | tf_op jit(solution)/shard_map/key_gradient/pallas_call | solution.py:240
  (19 shorter events, 0.1 us)
Async XLA Ops:
  1.6 6.4 %collective-permute-start = (bf16[2,128,384]{2,1,0:T(8,128)(2,1)S(1)}, bf16[2,128,384]{2,1,0:T(8,128)(2,1)S(1)}, u32[]{:S(2)}, u32[]{:S(2)}) collective-permute-start(bf16[2,128,384]{2,1,0:T(8,128)(2,1)S(1)} %pad_maximum_fusion.own), channel_id=1, source_target_pairs={{8,16},{12,20},{16,8},{20,12},{9,17},{13,21},{17,9},{21,13},{10,18... | collective-permute-start | bytes 589832 | tf_op jit(solution)/shard_map/ppermute | solution.py:277
  2.3 14.5 %collective-permute-start.1 = (bf16[2,128,384]{2,1,0:T(8,128)(2,1)S(1)}, bf16[2,128,384]{2,1,0:T(8,128)(2,1)S(1)}, u32[]{:S(2)}, u32[]{:S(2)}) collective-permute-start(bf16[2,128,384]{2,1,0:T(8,128)(2,1)S(1)} %pad_maximum_fusion.own), channel_id=1, source_target_pairs={{0,8},{4,12},{8,0},{12,4},{16,24},{20,28},{24,16},{28,20},{1,9},{5... | collective-permute-start | bytes 589832 | tf_op jit(solution)/shard_map/ppermute | solution.py:277
  8.0 11.8 %collective-permute-start.2 = (bf16[2,128,384]{2,1,0:T(8,128)(2,1)S(1)}, bf16[2,128,384]{2,1,0:T(8,128)(2,1)S(1)}, u32[]{:S(2)}, u32[]{:S(2)}) collective-permute-start(bf16[2,128,384]{2,1,0:T(8,128)(2,1)S(1)} %pad_maximum_fusion.own), channel_id=1, source_target_pairs={{0,4},{4,0},{8,12},{12,8},{16,20},{20,16},{24,28},{28,24},{1,5},{5... | collective-permute-start | bytes 589832 | tf_op jit(solution)/shard_map/ppermute | solution.py:277
  8.0 8.9 %copy-start = (bf16[128,384]{1,0:T(8,128)(2,1)S(1)}, bf16[128,384]{1,0:T(8,128)(2,1)}, u32[]{:S(2)}) copy-start(bf16[128,384]{1,0:T(8,128)(2,1)} %q0) | copy-start | bytes 294916
  8.0 11.8 %copy-start.3 = (f32[384]{0:T(512)S(1)}, f32[384]{0:T(512)}, u32[]{:S(2)}) copy-start(f32[384]{0:T(512)} %param.10) | copy-start | bytes 4612
  8.0 11.9 %copy-start.1 = (bf16[128,384]{1,0:T(8,128)(2,1)S(1)}, bf16[128,384]{1,0:T(8,128)(2,1)}, u32[]{:S(2)}) copy-start(bf16[128,384]{1,0:T(8,128)(2,1)} %g_ref.3) | copy-start | bytes 294916
  16.8 3.1 %copy-start.2 = (s32[1,4]{1,0:T(1,128)S(1)}, s32[1,4]{1,0:T(1,128)}, u32[]{:S(2)}) copy-start(s32[1,4]{1,0:T(1,128)} %flags_ref.5) | copy-start | bytes 52
  16.8 3.1 %collective-permute-start.3 = (bf16[2,128,384]{2,1,0:T(8,128)(2,1)S(1)}, bf16[2,128,384]{2,1,0:T(8,128)(2,1)S(1)}, u32[]{:S(2)}, u32[]{:S(2)}) collective-permute-start(bf16[2,128,384]{2,1,0:T(8,128)(2,1)S(1)} %broadcast_select_fusion), channel_id=1, source_target_pairs={{0,4},{4,0},{8,12},{12,8},{16,20},{20,16},{24,28},{28,24},{1,5},{5... | collective-permute-start | bytes 589832 | tf_op jit(solution)/shard_map/ppermute | solution.py:283
  16.9 10.5 %collective-permute-start.4 = (bf16[128,384]{1,0:T(8,128)(2,1)S(1)}, bf16[128,384]{1,0:T(8,128)(2,1)S(1)}, u32[]{:S(2)}, u32[]{:S(2)}) collective-permute-start(bf16[128,384]{1,0:T(8,128)(2,1)S(1)} %copy-done), channel_id=1, source_target_pairs={{8,16},{12,20},{16,8},{20,12},{9,17},{13,21},{17,9},{21,13},{10,18... | collective-permute-start | bytes 294920 | tf_op jit(solution)/shard_map/ppermute | solution.py:277
  17.6 9.9 %collective-permute-start.5 = (bf16[128,384]{1,0:T(8,128)(2,1)S(1)}, bf16[128,384]{1,0:T(8,128)(2,1)S(1)}, u32[]{:S(2)}, u32[]{:S(2)}) collective-permute-start(bf16[128,384]{1,0:T(8,128)(2,1)S(1)} %copy-done), channel_id=1, source_target_pairs={{0,8},{4,12},{8,0},{12,4},{16,24},{20,28},{24,16},{28,20},{1,9},{5... | collective-permute-start | bytes 294920 | tf_op jit(solution)/shard_map/ppermute | solution.py:277
  19.8 7.6 %collective-permute-start.6 = (bf16[128,384]{1,0:T(8,128)(2,1)S(1)}, bf16[128,384]{1,0:T(8,128)(2,1)S(1)}, u32[]{:S(2)}, u32[]{:S(2)}) collective-permute-start(bf16[128,384]{1,0:T(8,128)(2,1)S(1)} %copy-done), channel_id=1, source_target_pairs={{0,4},{4,0},{8,12},{12,8},{16,20},{20,16},{24,28},{28,24},{1,5},{5... | collective-permute-start | bytes 294920 | tf_op jit(solution)/shard_map/ppermute | solution.py:277
  22.5 10.5 %all-to-all-start = ((f32[4,8,128]{2,1,0:T(8,128)}), f32[4,8,128]{2,1,0:T(8,128)S(1)}, u32[]{:S(2)}, u32[]{:S(2)}) async-start(f32[4,8,128]{2,1,0:T(8,128)} %get-tuple-element.29.stats_ref), calls=%async_computation | async-start | bytes 32768 | tf_op jit(solution)/shard_map/all_to_all | solution.py:299
  34.1 6.4 %collective-permute-start.7 = (bf16[144,384]{1,0:T(8,128)(2,1)S(1)}, bf16[144,384]{1,0:T(8,128)(2,1)S(1)}, u32[]{:S(2)}, u32[]{:S(2)}) collective-permute-start(bf16[144,384]{1,0:T(8,128)(2,1)S(1)} %get-tuple-element.46.msg_ref.m0), channel_id=1, source_target_pairs={{8,16},{12,20},{16,8},{20,12},{9,17},{13,21},{17,9},{21,13},{10,18... | collective-permute-start | bytes 331784 | tf_op jit(solution)/shard_map/ppermute | solution.py:277
  34.8 7.2 %collective-permute-start.8 = (bf16[144,384]{1,0:T(8,128)(2,1)S(1)}, bf16[144,384]{1,0:T(8,128)(2,1)S(1)}, u32[]{:S(2)}, u32[]{:S(2)}) collective-permute-start(bf16[144,384]{1,0:T(8,128)(2,1)S(1)} %get-tuple-element.46.msg_ref.m0), channel_id=1, source_target_pairs={{0,8},{4,12},{8,0},{12,4},{16,24},{20,28},{24,16},{28,20},{1,9},{5... | collective-permute-start | bytes 331784 | tf_op jit(solution)/shard_map/ppermute | solution.py:277
  37.9 4.1 %collective-permute-start.9 = (bf16[144,384]{1,0:T(8,128)(2,1)S(1)}, bf16[144,384]{1,0:T(8,128)(2,1)S(1)}, u32[]{:S(2)}, u32[]{:S(2)}) collective-permute-start(bf16[144,384]{1,0:T(8,128)(2,1)S(1)} %get-tuple-element.46.msg_ref.m0), channel_id=1, source_target_pairs={{0,4},{4,0},{8,12},{12,8},{16,20},{20,16},{24,28},{28,24},{1,5},{5... | collective-permute-start | bytes 331784 | tf_op jit(solution)/shard_map/ppermute | solution.py:277
  37.9 2.6 %collective-permute-start.10 = (bf16[128,384]{1,0:T(8,128)(2,1)S(1)}, bf16[128,384]{1,0:T(8,128)(2,1)S(1)}, u32[]{:S(2)}, u32[]{:S(2)}) collective-permute-start(bf16[128,384]{1,0:T(8,128)(2,1)S(1)} %broadcast_select_fusion.2), channel_id=1, source_target_pairs={{0,4},{4,0},{8,12},{12,8},{16,20},{20,16},{24,28},{28,24},{1,5},{5... | collective-permute-start | bytes 294920 | tf_op jit(solution)/shard_map/ppermute | solution.py:283
  42.0 1.4 %collective-permute-start.11 = (bf16[144,384]{1,0:T(8,128)(2,1)S(1)}, bf16[144,384]{1,0:T(8,128)(2,1)S(1)}, u32[]{:S(2)}, u32[]{:S(2)}) collective-permute-start(bf16[144,384]{1,0:T(8,128)(2,1)S(1)} %broadcast_select_fusion.1), channel_id=1, source_target_pairs={{0,4},{4,0},{8,12},{12,8},{16,20},{20,16},{24,28},{28,24},{1,5},{5... | collective-permute-start | bytes 331784 | tf_op jit(solution)/shard_map/ppermute | solution.py:283
